TPU v7x, 512 devices: a whole 4x4x16 slice. The times are simulated.
512 devices in a mesh: tok: 2 (over core), head: 16 (over y, x), exp: 16 (over z).
Axes of the slice: x: 4, y: 4, z: 16, core: 2. Of those that a mesh axis runs over, the one named last changes fastest.
Arguments:
- context: bfloat16 [16, 64, 4096], P('exp', 'tok', 'head'), may hold values from -6 to 6
- out_proj: bfloat16 [4096, 4096], P('head', 'exp'), may hold values from -0.125 to 0.125
- stream: float32 [16, 64, 4096], P('exp', 'tok', 'head'), may hold values from -75 to 75
- norm_gain: float32 [4096], replicated, may hold values from 0.1 to 1.9
- expert_ids: int32 [16, 64, 8], P('exp', 'tok'), may hold values from 0 to 31, as said below
- slot_ids: int32 [16, 64, 8], P('exp', 'tok'), may hold values from -1 to 11, as said below
- gate_probs: float32 [16, 64, 8], P('exp', 'tok'), may hold values from 0.02 to 0.3
- w_gate: bfloat16 [32, 3072, 4096], P(('tok', 'exp'), 'head'), may hold values from -0.09375 to 0.09375
- w_up: bfloat16 [32, 3072, 4096], P(('tok', 'exp'), 'head'), may hold values from -0.09375 to 0.09375
- w_down: bfloat16 [32, 3072, 4096], P(('tok', 'exp'), 'head'), may hold values from -0.15625 to 0.15625
Outputs:
- mixed: float32 [16, 64, 4096], P('exp', 'tok', 'head')
Inputs may be any that keep to these rules, and one draw needn't show every extreme that they name: `expert_ids`: each token names 8 different experts. `slot_ids`: within a block of 32 consecutive tokens of one image, the choices of one expert take slots 0, 1, 2, ... in token order until its 12 slots are full, later ones get -1; in every block some expert fills all 12 slots.
All inputs are finite; a program needn't handle non-finite values.
Results may differ from a plain program's by a relative error of at most 0.0034.
Values may be sent and summed in bfloat16 or wider, within the bound.
No kernel may reach another device: no remote copies, remote signals or barrier semaphores. Data moves between devices by JAX's collectives and lax.ppermute only.
A program may use at most 64 MiB of HBM per device.

v0:
```python
import jax
import jax.numpy as jnp
from jax import lax
from jax.sharding import Mesh
from jax.sharding import PartitionSpec as P

EXPERTS = 32
TOP = 8
CAP = 12
HEAD = ("head_0", "head_1")
eps_value = 1e-05


def cut_along(x, dim, count):
    shape = x.shape
    pieces = x.reshape(*shape[:dim], count, shape[dim] // count, *shape[dim + 1 :])
    return jnp.moveaxis(pieces, dim, 0)


def sum_at_owner(x, axis, dim):
    pieces = cut_along(x, dim, lax.axis_size(axis))
    arrived = lax.all_to_all(pieces, axis, split_axis=0, concat_axis=0, tiled=True)
    return arrived.astype(jnp.float32).sum(axis=0)


def over_axes(x, axes):
    for axis in axes:
        x = lax.psum(x, axis)
    return x


def gather_axes(x, axes, dim):
    result = x
    for number in range(len(axes) - 1, -1, -1):
        result = lax.all_gather(result, axes[number], axis=dim, tiled=True)
    return result


def on_device(
    context, out_proj, stream, norm_gain, expert_ids, slot_ids, gate_probs, w_gate, w_up, w_down
):
    local_context = context[0]
    own_stream = stream[0]
    col_width = own_stream.shape[1]
    full_width = col_width * lax.axis_size(HEAD)
    col_start = lax.axis_index(HEAD) * col_width
    partial_value = jnp.dot(
        local_context,
        lax.all_gather(out_proj, "exp", axis=1, tiled=True),
        preferred_element_type=jnp.float32,
    )
    resid_own = sum_at_owner(partial_value.astype(jnp.bfloat16), HEAD, 1) + own_stream
    total_sq = over_axes(jnp.sum(resid_own * resid_own, axis=1, keepdims=True), HEAD)
    gain_own = lax.dynamic_slice_in_dim(norm_gain, col_start, col_width, 0)
    normed_own = (resid_own * lax.rsqrt(total_sq / full_width + eps_value) * gain_own).astype(
        jnp.bfloat16
    )
    choice_ids = expert_ids[0]
    choice_slots = slot_ids[0]
    weights = gate_probs[0]
    spill_slot = EXPERTS * CAP
    target = jnp.where(choice_slots >= 0, choice_ids * CAP + choice_slots, spill_slot)
    outgoing = (
        jnp.zeros((spill_slot + 1, col_width), jnp.bfloat16)
        .at[target.reshape(-1)]
        .set(jnp.repeat(normed_own, TOP, axis=0))
    )
    outgoing = outgoing[:spill_slot].reshape(EXPERTS, CAP, col_width)
    tok_count = lax.axis_size("tok")
    groups = tok_count * lax.axis_size("exp")
    local_experts = w_gate.shape[0]
    arrived = lax.all_to_all(outgoing, ("tok", "exp"), split_axis=0, concat_axis=0, tiled=True)
    arrived = arrived.reshape(groups, local_experts, CAP, col_width)
    piece = gather_axes(arrived, HEAD, 3)
    gate_more = jnp.einsum("slcd,lhd->slch", piece, w_gate, preferred_element_type=jnp.float32)
    up_more = jnp.einsum("slcd,lhd->slch", piece, w_up, preferred_element_type=jnp.float32)
    hidden = (jax.nn.silu(gate_more) * up_more).astype(jnp.bfloat16)
    produced = jnp.einsum(
        "slch,lhd->slcd", hidden, w_down, preferred_element_type=jnp.float32
    ).astype(jnp.bfloat16)
    widened = lax.optimization_barrier(produced).astype(jnp.float32)
    summed = sum_at_owner(widened.astype(jnp.bfloat16), HEAD, 3)
    returned_share = lax.all_to_all(
        summed.reshape(EXPERTS, CAP, col_width).astype(jnp.bfloat16),
        ("tok", "exp"),
        split_axis=0,
        concat_axis=0,
        tiled=True,
    ).astype(jnp.float32)
    lookup_share = jnp.concatenate(
        [returned_share.reshape(spill_slot, col_width), jnp.zeros((1, col_width), jnp.float32)],
        axis=0,
    )
    picked_share = lookup_share[target]
    expert_own = jnp.sum(picked_share * weights[:, :, None], axis=1)
    return (resid_own + expert_own)[None]


def solution(mesh):
    split = Mesh(
        mesh.devices.reshape(mesh.shape["tok"], 4, 4, mesh.shape["exp"]),
        ("tok", "head_0", "head_1", "exp"),
    )
    in_specs = (
        P("exp", "tok", HEAD),
        P(HEAD, "exp"),
        P("exp", "tok", HEAD),
        P(),
        P("exp", "tok", None),
        P("exp", "tok", None),
        P("exp", "tok", None),
        P(("tok", "exp"), HEAD, None),
        P(("tok", "exp"), HEAD, None),
        P(("tok", "exp"), HEAD, None),
    )
    out_specs = P("exp", "tok", HEAD)
    return jax.shard_map(
        on_device, mesh=split, in_specs=in_specs, out_specs=out_specs, check_vma=False
    )
```

profile of v0, /device:TPU:1, one launch (start us, length us, event | category | flops | bytes accessed | tf_op | source)
XLA Modules:
  0.0 316.5 jit_solution(14243525346558986769)
XLA Ops:
  6.6 0.7 all-gather.5.cloned.1.call-update
  7.3 76.2 %all-gather.5.cloned.1.call-done = bf16[256,4096]{1,0:T(8,128)(2,1)} async-done(((bf16[256,256]{1,0:T(8,128)(2,1)}), bf16[256,4096]{1,0:T(8,128)(2,1)}) %all-gather.5.cloned.1.call-update) | async-done | bytes 2097168 | tf_op jit(solution)/shard_map/all_gather | solution.py:49
  83.5 2.1 convolution_convert_fusion.1
  85.6 0.7 copy.38
  86.3 6.5 %all-to-all-start = ((bf16[16,32,256]{2,1,0:T(8,128)(2,1)}), bf16[16,32,256]{2,1,0:T(8,128)(2,1)S(1)}, u32[]{:S(2)}, u32[]{:S(2)}) async-start(bf16[16,32,256]{2,1,0:T(8,128)(2,1)} %bitcast.101), calls=%async_computation | async-start | bytes 524288 | tf_op jit(solution)/shard_map/all_to_all | solution.py:22
  93.1 0.8 dynamic_slice.3
  93.9 6.5 %all-to-all-done = bf16[16,32,256]{2,1,0:T(8,128)(2,1)S(1)} async-done(((bf16[16,32,256]{2,1,0:T(8,128)(2,1)}), bf16[16,32,256]{2,1,0:T(8,128)(2,1)S(1)}, u32[]{:S(2)}, u32[]{:S(2)}) %all-to-all-start) | async-done | bytes 262176 | tf_op jit(solution)/shard_map/all_to_all | solution.py:22
  100.5 6.6 %psum.14 = f32[32,1]{0,1:T(1,128)S(1)} all-reduce(f32[32,1]{0,1:T(1,128)S(1)} %bitcast.107), channel_id=1, replica_groups=mesh['tok'=2,'head_0'=4,'head_1'=4,'exp'=16] {'head_0'}, use_global_device_ids=true, to_apply=%region_2.0 | all-reduce | flops 32 | bytes 256 | tf_op jit(solution)/shard_map/psum | solution.py:28
  107.1 7.0 %psum.15 = f32[32,1]{0,1:T(1,128)S(1)} all-reduce(f32[32,1]{0,1:T(1,128)S(1)} %psum.14), channel_id=1, replica_groups=mesh['tok'=2,'head_0'=4,'head_1'=4,'exp'=16] {'head_1'}, use_global_device_ids=true, to_apply=%region_3.0 | all-reduce | flops 32 | bytes 256 | tf_op jit(solution)/shard_map/psum | solution.py:28
  114.2 1.5 scatter_custom_fusion
  115.8 44.8 %all_to_all.20 = bf16[32,12,256]{2,1,0:T(8,128)(2,1)S(1)} all-to-all(bf16[32,12,256]{2,1,0:T(8,128)(2,1)S(1)} %reshape.147), channel_id=1, replica_groups=mesh['tok'=2,'head_0'=4,'head_1'=4,'exp'=16] {'tok','exp'}, dimensions={0} | all-to-all | bytes 393216 | tf_op jit(solution)/shard_map/all_to_all | solution.py:72
  160.6 13.4 %all-gather = bf16[32,12,1024]{2,0,1:T(8,128)(2,1)} all-gather(bf16[32,12,256]{2,0,1:T(8,128)(2,1)S(1)} %copy.26), channel_id=2, replica_groups=mesh['tok'=2,'head_0'=4,'head_1'=4,'exp'=16] {'head_1'}, dimensions={2}, use_global_device_ids=true | all-gather | bytes 983040 | tf_op jit(solution)/shard_map/all_gather | solution.py:35
  174.0 36.9 %all-gather.7.cloned.1.call-done = bf16[32,12,4096]{2,0,1:T(8,128)(2,1)} async-done(((bf16[32,12,1024]{2,0,1:T(8,128)(2,1)}), bf16[32,12,4096]{2,0,1:T(8,128)(2,1)}) %all-gather.7.cloned.1.call-update) | async-done | bytes 3145744 | tf_op jit(solution)/shard_map/all_gather | solution.py:35
  210.9 3.7 %fusion.6 = f32[32,1,12,192]{3,0,2,1:T(8,128)} fusion(bf16[32,12,4096]{2,0,1:T(8,128)(2,1)} %all-gather.7.cloned.1.call-done, bf16[1,192,4096]{2,1,0:T(8,128)(2,1)S(1)} %copy-done.5), kind=kOutput, calls=%fused_computation.11 | convolution fusion | flops 603979776 | bytes 5013504 | tf_op jit(solution)/shard_map/slcd,lhd->slch/dot_general | solution.py:75
  214.6 7.6 %fusion = bf16[32,1,12,4096]{3,0,2,1:T(8,128)(2,1)} fusion(bf16[1,192,4096]{2,1,0:T(8,128)(2,1)S(1)} %copy-done, bf16[32,12,4096]{2,0,1:T(8,128)(2,1)} %all-gather.7.cloned.1.call-done, bf16[1,192,4096]{2,1,0:T(8,128)(2,1)} %param.18, f32[32,1,12,192]{3,0,2,1:T(8,128)} %fusion.6), kind=kOutput, calls=%fused_computation.3 | convolution fusion | flops 1209974784 | bytes 9732096 | tf_op jit(solution)/shard_map/slch,lhd->slcd/dot_general | solution.py:78
  222.2 2.3 copy.37
  224.5 44.0 %all_to_all.21 = bf16[16,32,1,12,256]{4,1,3,2,0:T(8,128)(2,1)} all-to-all(bf16[16,32,1,12,256]{4,1,3,2,0:T(8,128)(2,1)S(1)} %bitcast.102), channel_id=1, replica_groups=mesh['tok'=2,'head_0'=4,'head_1'=4,'exp'=16] {'head_0','head_1'}, dimensions={0} | all-to-all | bytes 6291456 | tf_op jit(solution)/shard_map/all_to_all | solution.py:22
  268.5 2.6 reduce_sum.46
  271.0 0.8 copy.29
  271.8 14.3 %all-to-all-start.3 = ((bf16[32,12,256]{2,1,0:T(8,128)(2,1)}), bf16[32,12,256]{2,1,0:T(8,128)(2,1)S(1)}, u32[]{:S(2)}, u32[]{:S(2)}) async-start(bf16[32,12,256]{2,1,0:T(8,128)(2,1)} %copy.29), calls=%async_computation.3 | async-start | bytes 524288 | tf_op jit(solution)/shard_map/all_to_all | solution.py:83
  286.4 21.4 %all-to-all-done.3 = bf16[32,12,256]{2,1,0:T(8,128)(2,1)S(1)} async-done(((bf16[32,12,256]{2,1,0:T(8,128)(2,1)}), bf16[32,12,256]{2,1,0:T(8,128)(2,1)S(1)}, u32[]{:S(2)}, u32[]{:S(2)}) %all-to-all-start.3) | async-done | bytes 196640 | tf_op jit(solution)/shard_map/all_to_all | solution.py:83
  307.9 1.0 gather_fusion
  308.9 0.1 fusion.28
  309.0 0.6 bitcast_add_fusion
  (32 shorter events, 1.0 us)
Async XLA Ops:
  6.5 208.1 %copy-start = (bf16[1,192,4096]{2,1,0:T(8,128)(2,1)S(1)}, bf16[1,192,4096]{2,1,0:T(8,128)(2,1)}, u32[]{:S(2)}) copy-start(bf16[1,192,4096]{2,1,0:T(8,128)(2,1)} %param.19) | copy-start | bytes 4718596
  6.5 86.4 %copy-start.4 = (s32[1,32,8]{1,2,0:T(8,128)S(1)}, s32[1,32,8]{1,2,0:T(8,128)}, u32[]{:S(2)}) copy-start(s32[1,32,8]{1,2,0:T(8,128)} %param.14) | copy-start | bytes 3076
  6.5 86.4 %copy-start.3 = (s32[1,32,8]{1,2,0:T(8,128)S(1)}, s32[1,32,8]{1,2,0:T(8,128)}, u32[]{:S(2)}) copy-start(s32[1,32,8]{1,2,0:T(8,128)} %param.15) | copy-start | bytes 3076
  6.5 93.9 %copy-start.1 = (f32[1,32,256]{2,1,0:T(8,128)S(1)}, f32[1,32,256]{2,1,0:T(8,128)}, u32[]{:S(2)}) copy-start(f32[1,32,256]{2,1,0:T(8,128)} %param.12) | copy-start | bytes 98308
  6.5 77.0 %all-gather.5.cloned.1.call-start = ((), (), s32[]{:S(2)}) async-start(), calls=%async_computation.4 | async-start | bytes 2228224 | tf_op jit(solution)/shard_map/all_gather | solution.py:49
  86.3 14.1 %all-to-all-start = ((bf16[16,32,256]{2,1,0:T(8,128)(2,1)}), bf16[16,32,256]{2,1,0:T(8,128)(2,1)S(1)}, u32[]{:S(2)}, u32[]{:S(2)}) async-start(bf16[16,32,256]{2,1,0:T(8,128)(2,1)} %bitcast.101), calls=%async_computation | async-start | bytes 524288 | tf_op jit(solution)/shard_map/all_to_all | solution.py:22
  92.8 118.1 %all-gather.7.cloned.1.call-start = ((), (), s32[]{:S(2)}) async-start(), calls=%async_computation.5 | async-start | bytes 3932160 | tf_op jit(solution)/shard_map/all_gather | solution.py:35
  115.8 95.2 %copy-start.5 = (bf16[1,192,4096]{2,1,0:T(8,128)(2,1)S(1)}, bf16[1,192,4096]{2,1,0:T(8,128)(2,1)}, u32[]{:S(2)}) copy-start(bf16[1,192,4096]{2,1,0:T(8,128)(2,1)} %param.17) | copy-start | bytes 4718596
  268.5 17.9 %copy-start.2 = (f32[1,32,8]{1,2,0:T(8,128)S(1)}, f32[1,32,8]{1,2,0:T(8,128)}, u32[]{:S(2)}) copy-start(f32[1,32,8]{1,2,0:T(8,128)} %param.16) | copy-start | bytes 3076
  271.8 36.0 %all-to-all-start.3 = ((bf16[32,12,256]{2,1,0:T(8,128)(2,1)}), bf16[32,12,256]{2,1,0:T(8,128)(2,1)S(1)}, u32[]{:S(2)}, u32[]{:S(2)}) async-start(bf16[32,12,256]{2,1,0:T(8,128)(2,1)} %copy.29), calls=%async_computation.3 | async-start | bytes 524288 | tf_op jit(solution)/shard_map/all_to_all | solution.py:83
Sparse Core Ops, SparseCore 0:
  9.4 74.0 all-gather.4
  174.2 36.7 all-gather.6
where the time goes:
time: 317 us; the launch traced here: 316 us
  waiting for transfers between devices  142 us (45%)
  blocking collectives  116 us (37%)
  starting transfers between devices  20.9 us (7%)
  between operations  13.6 us (4%)
  matrix products  13.3 us (4%)
  local copies, waits for them, and re-layouts  7.68 us (2%)
  other arithmetic  3.61 us (1%)
    all_gather x1, waiting for transfers between devices, on_device(): lax.all_gather(out_proj, 'exp', axis=1, tiled=True)  76.2 us
    all_to_all x1, blocking collectives, on_device(): lax.all_to_all(outgoing, ('tok', 'exp'), split_axis=0, concat_axis=0, til...  44.8 us
    all_to_all x1, blocking collectives, sum_at_owner(): lax.all_to_all(pieces, axis, split_axis=0, concat_axis=0, tiled=True)  44 us
    all_gather x1, waiting for transfers between devices, gather_axes(): result = lax.all_gather(result, axes[number], axis=dim, tiled=True)  36.9 us
    all_to_all x1, waiting for transfers between devices, on_device(): lax.all_to_all(summed.reshape(EXPERTS, CAP, col_width).astype(jnp.bfloat1...  21.4 us
    all_to_all x1, starting transfers between devices, on_device(): lax.all_to_all(summed.reshape(EXPERTS, CAP, col_width).astype(jnp.bfloat1...  14.3 us
    psum x2, blocking collectives, over_axes(): x = lax.psum(x, axis)  13.5 us
    all_gather x1, blocking collectives, gather_axes(): result = lax.all_gather(result, axes[number], axis=dim, tiled=True)  13.4 us
  transfers between devices with their start and end apart: 4, of which 4 were waited for; matrix products, arithmetic and copies ran while one was open for 0% of the time, Pallas kernels for 0%

commit v1 on v0

--- a/solution.py
+++ b/solution.py
@@ -9,6 +9,22 @@
 CAP = 12
 HEAD = ("head_0", "head_1")
 eps_value = 1e-05
+
+
+def ring_gather(x, axis, dim):
+    ways, here, step = (lax.axis_size(axis), lax.axis_index(axis), x.shape[dim])
+    lengths = [n * ways if d == dim else n for d, n in enumerate(x.shape)]
+    full = lax.dynamic_update_slice_in_dim(jnp.zeros(lengths, x.dtype), x, here * step, axis=dim)
+    going_up = going_down = x
+    for far in range(1, ways // 2 + 1):
+        going_up = lax.ppermute(going_up, axis, [(d, (d + 1) % ways) for d in range(ways)])
+        full = lax.dynamic_update_slice_in_dim(full, going_up, (here - far) % ways * step, axis=dim)
+        if 2 * far < ways:
+            going_down = lax.ppermute(going_down, axis, [(d, (d - 1) % ways) for d in range(ways)])
+            full = lax.dynamic_update_slice_in_dim(
+                full, going_down, (here + far) % ways * step, axis=dim
+            )
+    return full
 
 
 def cut_along(x, dim, count):
@@ -45,9 +61,7 @@
     full_width = col_width * lax.axis_size(HEAD)
     col_start = lax.axis_index(HEAD) * col_width
     partial_value = jnp.dot(
-        local_context,
-        lax.all_gather(out_proj, "exp", axis=1, tiled=True),
-        preferred_element_type=jnp.float32,
+        local_context, ring_gather(out_proj, "exp", 1), preferred_element_type=jnp.float32
     )
     resid_own = sum_at_owner(partial_value.astype(jnp.bfloat16), HEAD, 1) + own_stream
     total_sq = over_axes(jnp.sum(resid_own * resid_own, axis=1, keepdims=True), HEAD)

time: 317 us -> 305 us (0.962)
  waiting for transfers between devices: 142 us -> 74.7 us
  starting transfers between devices: 20.9 us -> 75.9 us
    all_gather x1 -> x0, waiting for transfers between devices: 76.2 us -> none  [on_device(): lax.all_gather(out_proj, 'exp', axis=1, tiled=True)]
    ppermute x0 -> x15, starting transfers between devices: none -> 54.8 us  [the longest x7 36.9 us: ring_gather(): lax.ppermute(going_down, axis, [(d, (d - 1) % ways) for d in range(ways)])]
    ppermute x0 -> x15, waiting for transfers between devices: none -> 9.87 us  [the longest x8 9.85 us: ring_gather(): lax.ppermute(going_up, axis, [(d, (d + 1) % ways) for d in range(ways)])]
  transfers between devices with their start and end apart: 4 -> 18, of which waited for: 4 -> 11; matrix products, arithmetic and copies ran while one was open for 0% -> 1% of each run, Pallas kernels for 0% -> 0%
where the time goes in v1:
time: 305 us; the launch traced here: 304 us
  blocking collectives  115 us (38%)
  starting transfers between devices  75.9 us (25%)
  waiting for transfers between devices  74.7 us (24%)
  between operations  14.2 us (5%)
  matrix products  11.6 us (4%)
  local copies, waits for them, and re-layouts  8.21 us (3%)
  other arithmetic  3.61 us (1%)
    all_to_all x1, blocking collectives, on_device(): lax.all_to_all(outgoing, ('tok', 'exp'), split_axis=0, concat_axis=0, til...  44.5 us
    all_to_all x1, blocking collectives, sum_at_owner(): lax.all_to_all(pieces, axis, split_axis=0, concat_axis=0, tiled=True)  44 us
    ppermute x7, starting transfers between devices, ring_gather(): lax.ppermute(going_down, axis, [(d, (d - 1) % ways) for d in range(ways)])  36.9 us
    all_gather x1, waiting for transfers between devices, gather_axes(): result = lax.all_gather(result, axes[number], axis=dim, tiled=True)  36.9 us
    all_to_all x1, waiting for transfers between devices, on_device(): lax.all_to_all(summed.reshape(EXPERTS, CAP, col_width).astype(jnp.bfloat1...  21.4 us
    ppermute x8, starting transfers between devices, ring_gather(): lax.ppermute(going_up, axis, [(d, (d + 1) % ways) for d in range(ways)])  17.9 us
    all_to_all x1, starting transfers between devices, on_device(): lax.all_to_all(summed.reshape(EXPERTS, CAP, col_width).astype(jnp.bfloat1...  14.3 us
    psum x2, blocking collectives, over_axes(): x = lax.psum(x, axis)  13.5 us
  transfers between devices with their start and end apart: 18, of which 11 were waited for; matrix products, arithmetic and copies ran while one was open for 1% of the time, Pallas kernels for 0%

profile of v1, /device:TPU:1, one launch (start us, length us, event | category | flops | bytes accessed | tf_op | source)
XLA Modules:
  0.0 303.7 jit_solution(3841631389184500405)
XLA Ops:
  6.5 4.5 %collective-permute-start = (bf16[256,256]{1,0:T(8,128)(2,1)}, bf16[256,256]{1,0:T(8,128)(2,1)S(1)}, u32[]{:S(2)}, u32[]{:S(2)}) collective-permute-start(bf16[256,256]{1,0:T(8,128)(2,1)} %param.11), channel_id=1, source_target_pairs={{0,1},{1,2},{2,3},{3,4},{4,5},{5,6},{6,7},{7,8},{8,9},{9,10},{10,1... | collective-permute-start | bytes 393224 | tf_op jit(solution)/shard_map/ppermute | solution.py:20
  11.0 9.5 %collective-permute-start.1 = (bf16[256,256]{1,0:T(8,128)(2,1)}, bf16[256,256]{1,0:T(8,128)(2,1)S(1)}, u32[]{:S(2)}, u32[]{:S(2)}) collective-permute-start(bf16[256,256]{1,0:T(8,128)(2,1)} %param.11), channel_id=1, source_target_pairs={{0,15},{1,0},{2,1},{3,2},{4,3},{5,4},{6,5},{7,6},{8,7},{9,8},{10,9... | collective-permute-start | bytes 393224 | tf_op jit(solution)/shard_map/ppermute | solution.py:23
  22.0 1.9 collective-permute-start.2
  24.0 4.6 %collective-permute-start.3 = (bf16[256,256]{1,0:T(8,128)(2,1)S(1)}, bf16[256,256]{1,0:T(8,128)(2,1)S(1)}, u32[]{:S(2)}, u32[]{:S(2)}) collective-permute-start(bf16[256,256]{1,0:T(8,128)(2,1)S(1)} %collective-permute-done.1), channel_id=1, source_target_pairs={{0,15},{1,0},{2,1},{3,2},{4,3},{5,4},{6,5},{7,6},{8,7},{9,8},{10,9... | collective-permute-start | bytes 393224 | tf_op jit(solution)/shard_map/ppermute | solution.py:23
  30.9 4.6 %collective-permute-start.5 = (bf16[256,256]{1,0:T(8,128)(2,1)S(1)}, bf16[256,256]{1,0:T(8,128)(2,1)S(1)}, u32[]{:S(2)}, u32[]{:S(2)}) collective-permute-start(bf16[256,256]{1,0:T(8,128)(2,1)S(1)} %collective-permute-done.3), channel_id=1, source_target_pairs={{0,15},{1,0},{2,1},{3,2},{4,3},{5,4},{6,5},{7,6},{8,7},{9,8},{10,9... | collective-permute-start | bytes 393224 | tf_op jit(solution)/shard_map/ppermute | solution.py:23
  37.8 4.6 %collective-permute-start.7 = (bf16[256,256]{1,0:T(8,128)(2,1)S(1)}, bf16[256,256]{1,0:T(8,128)(2,1)S(1)}, u32[]{:S(2)}, u32[]{:S(2)}) collective-permute-start(bf16[256,256]{1,0:T(8,128)(2,1)S(1)} %collective-permute-done.5), channel_id=1, source_target_pairs={{0,15},{1,0},{2,1},{3,2},{4,3},{5,4},{6,5},{7,6},{8,7},{9,8},{10,9... | collective-permute-start | bytes 393224 | tf_op jit(solution)/shard_map/ppermute | solution.py:23
  44.7 4.6 %collective-permute-start.9 = (bf16[256,256]{1,0:T(8,128)(2,1)S(1)}, bf16[256,256]{1,0:T(8,128)(2,1)S(1)}, u32[]{:S(2)}, u32[]{:S(2)}) collective-permute-start(bf16[256,256]{1,0:T(8,128)(2,1)S(1)} %collective-permute-done.7), channel_id=1, source_target_pairs={{0,15},{1,0},{2,1},{3,2},{4,3},{5,4},{6,5},{7,6},{8,7},{9,8},{10,9... | collective-permute-start | bytes 393224 | tf_op jit(solution)/shard_map/ppermute | solution.py:23
  51.6 4.6 %collective-permute-start.11 = (bf16[256,256]{1,0:T(8,128)(2,1)S(1)}, bf16[256,256]{1,0:T(8,128)(2,1)S(1)}, u32[]{:S(2)}, u32[]{:S(2)}) collective-permute-start(bf16[256,256]{1,0:T(8,128)(2,1)S(1)} %collective-permute-done.9), channel_id=1, source_target_pairs={{0,15},{1,0},{2,1},{3,2},{4,3},{5,4},{6,5},{7,6},{8,7},{9,8},{10,9... | collective-permute-start | bytes 393224 | tf_op jit(solution)/shard_map/ppermute | solution.py:23
  58.5 4.6 %collective-permute-start.13 = (bf16[256,256]{1,0:T(8,128)(2,1)S(1)}, bf16[256,256]{1,0:T(8,128)(2,1)S(1)}, u32[]{:S(2)}, u32[]{:S(2)}) collective-permute-start(bf16[256,256]{1,0:T(8,128)(2,1)S(1)} %collective-permute-done.11), channel_id=1, source_target_pairs={{0,15},{1,0},{2,1},{3,2},{4,3},{5,4},{6,5},{7,6},{8,7},{9,8},{10,9... | collective-permute-start | bytes 393224 | tf_op jit(solution)/shard_map/ppermute | solution.py:23
  66.3 6.1 %collective-permute-done.14 = bf16[256,256]{1,0:T(8,128)(2,1)S(1)} collective-permute-done((bf16[256,256]{1,0:T(8,128)(2,1)S(1)}, bf16[256,256]{1,0:T(8,128)(2,1)S(1)}, u32[]{:S(2)}, u32[]{:S(2)}) %collective-permute-start.14) | collective-permute-done | bytes 131104 | tf_op jit(solution)/shard_map/ppermute | solution.py:20
  73.6 6.8 %all-to-all-start = ((bf16[16,32,256]{2,1,0:T(8,128)(2,1)}), bf16[16,32,256]{2,1,0:T(8,128)(2,1)S(1)}, u32[]{:S(2)}, u32[]{:S(2)}) async-start(bf16[16,32,256]{2,1,0:T(8,128)(2,1)} %bitcast.102), calls=%async_computation | async-start | bytes 524288 | tf_op jit(solution)/shard_map/all_to_all | solution.py:38
  81.4 6.5 %all-to-all-done = bf16[16,32,256]{2,1,0:T(8,128)(2,1)S(1)} async-done(((bf16[16,32,256]{2,1,0:T(8,128)(2,1)}), bf16[16,32,256]{2,1,0:T(8,128)(2,1)S(1)}, u32[]{:S(2)}, u32[]{:S(2)}) %all-to-all-start) | async-done | bytes 262176 | tf_op jit(solution)/shard_map/all_to_all | solution.py:38
  88.1 7.2 %psum.14 = f32[32,1]{0,1:T(1,128)S(1)} all-reduce(f32[32,1]{0,1:T(1,128)S(1)} %bitcast.108), channel_id=1, replica_groups=mesh['tok'=2,'head_0'=4,'head_1'=4,'exp'=16] {'head_0'}, use_global_device_ids=true, to_apply=%region_2.3 | all-reduce | flops 32 | bytes 256 | tf_op jit(solution)/shard_map/psum | solution.py:44
  95.3 6.3 %psum.15 = f32[32,1]{0,1:T(1,128)S(1)} all-reduce(f32[32,1]{0,1:T(1,128)S(1)} %psum.14), channel_id=1, replica_groups=mesh['tok'=2,'head_0'=4,'head_1'=4,'exp'=16] {'head_1'}, use_global_device_ids=true, to_apply=%region_3.4 | all-reduce | flops 32 | bytes 256 | tf_op jit(solution)/shard_map/psum | solution.py:44
  103.3 44.5 %all_to_all.20 = bf16[32,12,256]{2,1,0:T(8,128)(2,1)S(1)} all-to-all(bf16[32,12,256]{2,1,0:T(8,128)(2,1)S(1)} %reshape.147), channel_id=1, replica_groups=mesh['tok'=2,'head_0'=4,'head_1'=4,'exp'=16] {'tok','exp'}, dimensions={0} | all-to-all | bytes 393216 | tf_op jit(solution)/shard_map/all_to_all | solution.py:86
  147.8 13.4 %all-gather = bf16[32,12,1024]{2,0,1:T(8,128)(2,1)} all-gather(bf16[32,12,256]{2,0,1:T(8,128)(2,1)S(1)} %copy.26), channel_id=2, replica_groups=mesh['tok'=2,'head_0'=4,'head_1'=4,'exp'=16] {'head_1'}, dimensions={2}, use_global_device_ids=true | all-gather | bytes 983040 | tf_op jit(solution)/shard_map/all_gather | solution.py:51
  161.2 36.9 %all-gather.4.cloned.1.call-done = bf16[32,12,4096]{2,0,1:T(8,128)(2,1)} async-done(((bf16[32,12,1024]{2,0,1:T(8,128)(2,1)}), bf16[32,12,4096]{2,0,1:T(8,128)(2,1)}) %all-gather.4.cloned.1.call-update) | async-done | bytes 3145744 | tf_op jit(solution)/shard_map/all_gather | solution.py:51
  198.1 3.6 %fusion.6 = f32[32,1,12,192]{3,0,2,1:T(8,128)} fusion(bf16[32,12,4096]{2,0,1:T(8,128)(2,1)} %all-gather.4.cloned.1.call-done, bf16[1,192,4096]{2,1,0:T(8,128)(2,1)S(1)} %copy-done.7), kind=kOutput, calls=%fused_computation.11 | convolution fusion | flops 603979776 | bytes 5013504 | tf_op jit(solution)/shard_map/slcd,lhd->slch/dot_general | solution.py:89
  201.8 7.5 %fusion = bf16[32,1,12,4096]{3,0,2,1:T(8,128)(2,1)} fusion(bf16[1,192,4096]{2,1,0:T(8,128)(2,1)S(1)} %copy-done, bf16[32,12,4096]{2,0,1:T(8,128)(2,1)} %all-gather.4.cloned.1.call-done, bf16[1,192,4096]{2,1,0:T(8,128)(2,1)} %param.18, f32[32,1,12,192]{3,0,2,1:T(8,128)} %fusion.6), kind=kOutput, calls=%fused_computation.3 | convolution fusion | flops 1209974784 | bytes 9732096 | tf_op jit(solution)/shard_map/slch,lhd->slcd/dot_general | solution.py:92
  209.3 2.3 copy.37
  211.6 44.0 %all_to_all.21 = bf16[16,32,1,12,256]{4,1,3,2,0:T(8,128)(2,1)} all-to-all(bf16[16,32,1,12,256]{4,1,3,2,0:T(8,128)(2,1)S(1)} %bitcast.103), channel_id=1, replica_groups=mesh['tok'=2,'head_0'=4,'head_1'=4,'exp'=16] {'head_0','head_1'}, dimensions={0} | all-to-all | bytes 6291456 | tf_op jit(solution)/shard_map/all_to_all | solution.py:38
  255.6 2.6 reduce_sum.46
  259.0 14.3 %all-to-all-start.3 = ((bf16[32,12,256]{2,1,0:T(8,128)(2,1)}), bf16[32,12,256]{2,1,0:T(8,128)(2,1)S(1)}, u32[]{:S(2)}, u32[]{:S(2)}) async-start(bf16[32,12,256]{2,1,0:T(8,128)(2,1)} %copy.29), calls=%async_computation.3 | async-start | bytes 524288 | tf_op jit(solution)/shard_map/all_to_all | solution.py:97
  273.6 21.4 %all-to-all-done.3 = bf16[32,12,256]{2,1,0:T(8,128)(2,1)S(1)} async-done(((bf16[32,12,256]{2,1,0:T(8,128)(2,1)}), bf16[32,12,256]{2,1,0:T(8,128)(2,1)S(1)}, u32[]{:S(2)}, u32[]{:S(2)}) %all-to-all-start.3) | async-done | bytes 196640 | tf_op jit(solution)/shard_map/all_to_all | solution.py:97
  (80 shorter events, 22.7 us)
Async XLA Ops:
  6.5 195.2 %copy-start = (bf16[1,192,4096]{2,1,0:T(8,128)(2,1)S(1)}, bf16[1,192,4096]{2,1,0:T(8,128)(2,1)}, u32[]{:S(2)}) copy-start(bf16[1,192,4096]{2,1,0:T(8,128)(2,1)} %param.19) | copy-start | bytes 4718596
  6.5 15.5 %collective-permute-start = (bf16[256,256]{1,0:T(8,128)(2,1)}, bf16[256,256]{1,0:T(8,128)(2,1)S(1)}, u32[]{:S(2)}, u32[]{:S(2)}) collective-permute-start(bf16[256,256]{1,0:T(8,128)(2,1)} %param.11), channel_id=1, source_target_pairs={{0,1},{1,2},{2,3},{3,4},{4,5},{5,6},{6,7},{7,8},{8,9},{9,10},{10,1... | collective-permute-start | bytes 393224 | tf_op jit(solution)/shard_map/ppermute | solution.py:20
  11.0 12.9 %collective-permute-start.1 = (bf16[256,256]{1,0:T(8,128)(2,1)}, bf16[256,256]{1,0:T(8,128)(2,1)S(1)}, u32[]{:S(2)}, u32[]{:S(2)}) collective-permute-start(bf16[256,256]{1,0:T(8,128)(2,1)} %param.11), channel_id=1, source_target_pairs={{0,15},{1,0},{2,1},{3,2},{4,3},{5,4},{6,5},{7,6},{8,7},{9,8},{10,9... | collective-permute-start | bytes 393224 | tf_op jit(solution)/shard_map/ppermute | solution.py:23
  21.1 51.3 %copy-start.3 = (bf16[1,32,256]{2,1,0:T(8,128)(2,1)S(1)}, bf16[1,32,256]{2,1,0:T(8,128)(2,1)}, u32[]{:S(2)}) copy-start(bf16[1,32,256]{2,1,0:T(8,128)(2,1)} %param.10) | copy-start | bytes 49156
  22.0 6.9 %collective-permute-start.2 = (bf16[256,256]{1,0:T(8,128)(2,1)S(1)}, bf16[256,256]{1,0:T(8,128)(2,1)S(1)}, u32[]{:S(2)}, u32[]{:S(2)}) collective-permute-start(bf16[256,256]{1,0:T(8,128)(2,1)S(1)} %collective-permute-done), channel_id=1, source_target_pairs={{0,1},{1,2},{2,3},{3,4},{4,5},{5,6},{6,7},{7,8},{8,9},{9,10},{10,1... | collective-permute-start | bytes 393224 | tf_op jit(solution)/shard_map/ppermute | solution.py:20
  24.0 6.9 %collective-permute-start.3 = (bf16[256,256]{1,0:T(8,128)(2,1)S(1)}, bf16[256,256]{1,0:T(8,128)(2,1)S(1)}, u32[]{:S(2)}, u32[]{:S(2)}) collective-permute-start(bf16[256,256]{1,0:T(8,128)(2,1)S(1)} %collective-permute-done.1), channel_id=1, source_target_pairs={{0,15},{1,0},{2,1},{3,2},{4,3},{5,4},{6,5},{7,6},{8,7},{9,8},{10,9... | collective-permute-start | bytes 393224 | tf_op jit(solution)/shard_map/ppermute | solution.py:23
  28.9 6.9 %collective-permute-start.4 = (bf16[256,256]{1,0:T(8,128)(2,1)S(1)}, bf16[256,256]{1,0:T(8,128)(2,1)S(1)}, u32[]{:S(2)}, u32[]{:S(2)}) collective-permute-start(bf16[256,256]{1,0:T(8,128)(2,1)S(1)} %collective-permute-done.2), channel_id=1, source_target_pairs={{0,1},{1,2},{2,3},{3,4},{4,5},{5,6},{6,7},{7,8},{8,9},{9,10},{10,1... | collective-permute-start | bytes 393224 | tf_op jit(solution)/shard_map/ppermute | solution.py:20
  30.9 6.9 %collective-permute-start.5 = (bf16[256,256]{1,0:T(8,128)(2,1)S(1)}, bf16[256,256]{1,0:T(8,128)(2,1)S(1)}, u32[]{:S(2)}, u32[]{:S(2)}) collective-permute-start(bf16[256,256]{1,0:T(8,128)(2,1)S(1)} %collective-permute-done.3), channel_id=1, source_target_pairs={{0,15},{1,0},{2,1},{3,2},{4,3},{5,4},{6,5},{7,6},{8,7},{9,8},{10,9... | collective-permute-start | bytes 393224 | tf_op jit(solution)/shard_map/ppermute | solution.py:23
  35.9 6.9 %collective-permute-start.6 = (bf16[256,256]{1,0:T(8,128)(2,1)S(1)}, bf16[256,256]{1,0:T(8,128)(2,1)S(1)}, u32[]{:S(2)}, u32[]{:S(2)}) collective-permute-start(bf16[256,256]{1,0:T(8,128)(2,1)S(1)} %collective-permute-done.4), channel_id=1, source_target_pairs={{0,1},{1,2},{2,3},{3,4},{4,5},{5,6},{6,7},{7,8},{8,9},{9,10},{10,1... | collective-permute-start | bytes 393224 | tf_op jit(solution)/shard_map/ppermute | solution.py:20
  37.8 6.9 %collective-permute-start.7 = (bf16[256,256]{1,0:T(8,128)(2,1)S(1)}, bf16[256,256]{1,0:T(8,128)(2,1)S(1)}, u32[]{:S(2)}, u32[]{:S(2)}) collective-permute-start(bf16[256,256]{1,0:T(8,128)(2,1)S(1)} %collective-permute-done.5), channel_id=1, source_target_pairs={{0,15},{1,0},{2,1},{3,2},{4,3},{5,4},{6,5},{7,6},{8,7},{9,8},{10,9... | collective-permute-start | bytes 393224 | tf_op jit(solution)/shard_map/ppermute | solution.py:23
  42.8 6.9 %collective-permute-start.8 = (bf16[256,256]{1,0:T(8,128)(2,1)S(1)}, bf16[256,256]{1,0:T(8,128)(2,1)S(1)}, u32[]{:S(2)}, u32[]{:S(2)}) collective-permute-start(bf16[256,256]{1,0:T(8,128)(2,1)S(1)} %collective-permute-done.6), channel_id=1, source_target_pairs={{0,1},{1,2},{2,3},{3,4},{4,5},{5,6},{6,7},{7,8},{8,9},{9,10},{10,1... | collective-permute-start | bytes 393224 | tf_op jit(solution)/shard_map/ppermute | solution.py:20
  44.7 6.9 %collective-permute-start.9 = (bf16[256,256]{1,0:T(8,128)(2,1)S(1)}, bf16[256,256]{1,0:T(8,128)(2,1)S(1)}, u32[]{:S(2)}, u32[]{:S(2)}) collective-permute-start(bf16[256,256]{1,0:T(8,128)(2,1)S(1)} %collective-permute-done.7), channel_id=1, source_target_pairs={{0,15},{1,0},{2,1},{3,2},{4,3},{5,4},{6,5},{7,6},{8,7},{9,8},{10,9... | collective-permute-start | bytes 393224 | tf_op jit(solution)/shard_map/ppermute | solution.py:23
  49.7 6.9 %collective-permute-start.10 = (bf16[256,256]{1,0:T(8,128)(2,1)S(1)}, bf16[256,256]{1,0:T(8,128)(2,1)S(1)}, u32[]{:S(2)}, u32[]{:S(2)}) collective-permute-start(bf16[256,256]{1,0:T(8,128)(2,1)S(1)} %collective-permute-done.8), channel_id=1, source_target_pairs={{0,1},{1,2},{2,3},{3,4},{4,5},{5,6},{6,7},{7,8},{8,9},{9,10},{10,1... | collective-permute-start | bytes 393224 | tf_op jit(solution)/shard_map/ppermute | solution.py:20
  51.6 6.9 %collective-permute-start.11 = (bf16[256,256]{1,0:T(8,128)(2,1)S(1)}, bf16[256,256]{1,0:T(8,128)(2,1)S(1)}, u32[]{:S(2)}, u32[]{:S(2)}) collective-permute-start(bf16[256,256]{1,0:T(8,128)(2,1)S(1)} %collective-permute-done.9), channel_id=1, source_target_pairs={{0,15},{1,0},{2,1},{3,2},{4,3},{5,4},{6,5},{7,6},{8,7},{9,8},{10,9... | collective-permute-start | bytes 393224 | tf_op jit(solution)/shard_map/ppermute | solution.py:23
  56.6 7.7 %collective-permute-start.12 = (bf16[256,256]{1,0:T(8,128)(2,1)S(1)}, bf16[256,256]{1,0:T(8,128)(2,1)S(1)}, u32[]{:S(2)}, u32[]{:S(2)}) collective-permute-start(bf16[256,256]{1,0:T(8,128)(2,1)S(1)} %collective-permute-done.10), channel_id=1, source_target_pairs={{0,1},{1,2},{2,3},{3,4},{4,5},{5,6},{6,7},{7,8},{8,9},{9,10},{10,1... | collective-permute-start | bytes 393224 | tf_op jit(solution)/shard_map/ppermute | solution.py:20
  58.5 7.7 %collective-permute-start.13 = (bf16[256,256]{1,0:T(8,128)(2,1)S(1)}, bf16[256,256]{1,0:T(8,128)(2,1)S(1)}, u32[]{:S(2)}, u32[]{:S(2)}) collective-permute-start(bf16[256,256]{1,0:T(8,128)(2,1)S(1)} %collective-permute-done.11), channel_id=1, source_target_pairs={{0,15},{1,0},{2,1},{3,2},{4,3},{5,4},{6,5},{7,6},{8,7},{9,8},{10,9... | collective-permute-start | bytes 393224 | tf_op jit(solution)/shard_map/ppermute | solution.py:23
  63.2 17.2 %copy-start.5 = (s32[1,32,8]{1,2,0:T(8,128)S(1)}, s32[1,32,8]{1,2,0:T(8,128)}, u32[]{:S(2)}) copy-start(s32[1,32,8]{1,2,0:T(8,128)} %param.15) | copy-start | bytes 3076
  64.3 8.1 %collective-permute-start.14 = (bf16[256,256]{1,0:T(8,128)(2,1)S(1)}, bf16[256,256]{1,0:T(8,128)(2,1)S(1)}, u32[]{:S(2)}, u32[]{:S(2)}) collective-permute-start(bf16[256,256]{1,0:T(8,128)(2,1)S(1)} %collective-permute-done.12), channel_id=1, source_target_pairs={{0,1},{1,2},{2,3},{3,4},{4,5},{5,6},{6,7},{7,8},{8,9},{9,10},{10,1... | collective-permute-start | bytes 393224 | tf_op jit(solution)/shard_map/ppermute | solution.py:20
  66.3 21.7 %copy-start.1 = (f32[1,32,256]{2,1,0:T(8,128)S(1)}, f32[1,32,256]{2,1,0:T(8,128)}, u32[]{:S(2)}) copy-start(f32[1,32,256]{2,1,0:T(8,128)} %param.12) | copy-start | bytes 98308
  73.6 14.3 %all-to-all-start = ((bf16[16,32,256]{2,1,0:T(8,128)(2,1)}), bf16[16,32,256]{2,1,0:T(8,128)(2,1)S(1)}, u32[]{:S(2)}, u32[]{:S(2)}) async-start(bf16[16,32,256]{2,1,0:T(8,128)(2,1)} %bitcast.102), calls=%async_computation | async-start | bytes 524288 | tf_op jit(solution)/shard_map/all_to_all | solution.py:38
  80.3 117.8 %all-gather.4.cloned.1.call-start = ((), (), s32[]{:S(2)}) async-start(), calls=%async_computation.4 | async-start | bytes 3932160 | tf_op jit(solution)/shard_map/all_gather | solution.py:51
  103.3 94.9 %copy-start.7 = (bf16[1,192,4096]{2,1,0:T(8,128)(2,1)S(1)}, bf16[1,192,4096]{2,1,0:T(8,128)(2,1)}, u32[]{:S(2)}) copy-start(bf16[1,192,4096]{2,1,0:T(8,128)(2,1)} %param.17) | copy-start | bytes 4718596
  255.6 17.9 %copy-start.4 = (f32[1,32,8]{1,2,0:T(8,128)S(1)}, f32[1,32,8]{1,2,0:T(8,128)}, u32[]{:S(2)}) copy-start(f32[1,32,8]{1,2,0:T(8,128)} %param.16) | copy-start | bytes 3076
  259.0 36.0 %all-to-all-start.3 = ((bf16[32,12,256]{2,1,0:T(8,128)(2,1)}), bf16[32,12,256]{2,1,0:T(8,128)(2,1)S(1)}, u32[]{:S(2)}, u32[]{:S(2)}) async-start(bf16[32,12,256]{2,1,0:T(8,128)(2,1)} %copy.29), calls=%async_computation.3 | async-start | bytes 524288 | tf_op jit(solution)/shard_map/all_to_all | solution.py:97
  (2 other events, 31.8 us)
Sparse Core Ops, SparseCore 0:
  161.4 36.7 all-gather.3
